TPU v7x, 128 devices: a whole 4x4x4 slice. The times are simulated.
128 devices in a mesh: rep: 2 (over y_hi), shard: 64 (over z, x, y_lo, core).
Axes of the slice: x: 4, y: 4 (y_hi: 2, y_lo: 2; y = y_hi * 2 + y_lo), z: 4, core: 2. Of those that a mesh axis runs over, the one named last changes fastest.
Arguments:
- tokens: bfloat16 [32768, 1024], P(('rep', 'shard')), may hold values from -6 to 6
- cotangent: bfloat16 [32768, 1024], P(('rep', 'shard')), may hold values from -6 to 6
- seq_lengths: int32 [512], replicated, may hold values from 0 to 256, as said below
- seq_device: int32 [512], replicated, may hold values from 0 to 127, as said below
- in_weight: float32 [1024, 3072], P('shard'), may hold values from -0.1875 to 0.1875
- conv_kernel: float32 [1024, 3], P('shard'), may hold values from -3.5 to 3.5
- out_weight: float32 [1024, 1024], P('shard'), may hold values from -0.1875 to 0.1875
- norm_gain: float32 [1024], P('shard'), may hold values from 0.5 to 1.5
- gate_weight: float32 [1024, 4608], P('shard'), may hold values from -0.1875 to 0.1875
- up_weight: float32 [1024, 4608], P('shard'), may hold values from -0.1875 to 0.1875
- down_weight: float32 [4608, 1024], P('shard'), may hold values from -0.09375 to 0.09375
- moment_in: float32 [1024, 3072], P('shard'), may hold values from -96 to 96
- moment_conv: float32 [1024, 3], P('shard'), may hold values from -128 to 128
- moment_out: float32 [1024, 1024], P('shard'), may hold values from -96 to 96
- moment_gain: float32 [1024], P('shard'), may hold values from -96 to 96
- moment_gate: float32 [1024, 4608], P('shard'), may hold values from -32 to 32
- moment_up: float32 [1024, 4608], P('shard'), may hold values from -32 to 32
- moment_down: float32 [4608, 1024], P('shard'), may hold values from -64 to 64
- square_in: float32 [1024, 3072], P('shard'), may hold values from 1310.72 to 5242.88
- square_conv: float32 [1024, 3], P('shard'), may hold values from 1900.544 to 7536.64
- square_out: float32 [1024, 1024], P('shard'), may hold values from 1310.72 to 5242.88
- square_gain: float32 [1024], P('shard'), may hold values from 1048.576 to 4259.84
- square_gate: float32 [1024, 4608], P('shard'), may hold values from 117.9648 to 471.8592
- square_up: float32 [1024, 4608], P('shard'), may hold values from 117.9648 to 471.8592
- square_down: float32 [4608, 1024], P('shard'), may hold values from 471.8592 to 1900.544
Outputs:
- block_out: bfloat16 [32768, 1024], P(('rep', 'shard'))
- input_grad: float32 [32768, 1024], P(('rep', 'shard'))
- updated_in: float32 [1024, 3072], P('shard')
- updated_conv: float32 [1024, 3], P('shard')
- updated_out: float32 [1024, 1024], P('shard')
- updated_gain: float32 [1024], P('shard')
- updated_gate: float32 [1024, 4608], P('shard')
- updated_up: float32 [1024, 4608], P('shard')
- updated_down: float32 [4608, 1024], P('shard')
- first_in: float32 [1024, 3072], P('shard')
- first_conv: float32 [1024, 3], P('shard')
- first_out: float32 [1024, 1024], P('shard')
- first_gain: float32 [1024], P('shard')
- first_gate: float32 [1024, 4608], P('shard')
- first_up: float32 [1024, 4608], P('shard')
- first_down: float32 [4608, 1024], P('shard')
- second_in: float32 [1024, 3072], P('shard')
- second_conv: float32 [1024, 3], P('shard')
- second_out: float32 [1024, 1024], P('shard')
- second_gain: float32 [1024], P('shard')
- second_gate: float32 [1024, 4608], P('shard')
- second_up: float32 [1024, 4608], P('shard')
- second_down: float32 [4608, 1024], P('shard')
Inputs may be any that keep to these rules, and one draw needn't show every extreme that they name: `seq_lengths`: the lengths of the entries of one device sum to between 128 and 256; a length of 0 marks an unused entry; some device holds a single sequence of 256 rows. `seq_device`: every device is named by exactly 4 entries.
All inputs are finite; a program needn't handle non-finite values.
Results may differ from a plain program's by a relative error of at most 0.011.
Values may be sent and summed in bfloat16 or wider, within the bound.
No kernel may reach another device: no remote copies, remote signals or barrier semaphores. Data moves between devices by JAX's collectives and lax.ppermute only.
A program may use at most 256 MiB of HBM per device.

v0:
```python
import jax
import jax.numpy as jnp
from jax import lax
from jax.sharding import PartitionSpec as P

STEP = 10


NORM_EPS = 1e-05
BETA_ONE = 0.9
BETA_TWO = 0.95
ADAM_EPS = 1e-08
STEP_RATES = (0.02, 0.3, 0.02, 0.3, 0.02, 0.02, 0.02)
DECAY_RATES = (0.1, 0.0, 0.1, 0.0, 0.1, 0.1, 0.1)


def layout(seq_lengths, seq_device, device, row_count):
    owned_len = jnp.where(seq_device == device, seq_lengths, 0)
    seq_ends = jnp.cumsum(owned_len, dtype=jnp.int32)
    slot_index = jnp.arange(row_count, dtype=jnp.int32)
    segment = jnp.sum(
        (seq_ends[None, :] <= slot_index[:, None]).astype(jnp.int32), axis=1, dtype=jnp.int32
    )
    live_rows = (slot_index < seq_ends[-1]).astype(jnp.int32)
    return (segment, live_rows)


def product(left, right):
    return jnp.dot(left, right, preferred_element_type=jnp.float32)


def product_nt(left, right):
    return lax.dot_general(
        left, right, (((1,), (1,)), ((), ())), preferred_element_type=jnp.float32
    )


def product_tn(left, right):
    return lax.dot_general(
        left, right, (((0,), (0,)), ((), ())), preferred_element_type=jnp.float32
    )


def conv_forward(mixed, kernel, segment):
    summed = mixed * kernel[:, 0]
    matches = []
    for offset in range(1, kernel.shape[1]):
        earlier = jnp.pad(mixed, ((offset, 0), (0, 0)))[:-offset]
        same_seq = (jnp.pad(segment, (offset, 0), constant_values=-1)[:-offset] == segment)[:, None]
        matches.append(same_seq)
        summed = summed + jnp.where(same_seq, earlier * kernel[:, offset], 0.0)
    return (summed, matches)


def conv_backward(gradient, mixed, kernel, matches):
    grad_mixed = gradient * kernel[:, 0]
    grad_taps = [jnp.sum(gradient * mixed, axis=0)]
    for offset in range(1, kernel.shape[1]):
        masked = jnp.where(matches[offset - 1], gradient, 0.0)
        later = jnp.pad(masked, ((0, offset), (0, 0)))[offset:]
        grad_mixed = grad_mixed + later * kernel[:, offset]
        earlier = jnp.pad(mixed, ((offset, 0), (0, 0)))[:-offset]
        grad_taps.append(jnp.sum(masked * earlier, axis=0))
    return (grad_mixed, jnp.stack(grad_taps, axis=1))


def body(
    tokens,
    cotangent,
    seq_lengths,
    seq_device,
    in_weight,
    conv_kernel,
    out_weight,
    norm_gain,
    gate_weight,
    up_weight,
    down_weight,
    moment_in,
    moment_conv,
    moment_out,
    moment_gain,
    moment_gate,
    moment_up,
    moment_down,
    square_in,
    square_conv,
    square_out,
    square_gain,
    square_gate,
    square_up,
    square_down,
):
    masters = (in_weight, conv_kernel, out_weight, norm_gain, gate_weight, up_weight, down_weight)
    moments = (moment_in, moment_conv, moment_out, moment_gain, moment_gate, moment_up, moment_down)
    squares = (square_in, square_conv, square_out, square_gain, square_gate, square_up, square_down)
    device = lax.axis_index("rep") * lax.axis_size("shard") + lax.axis_index("shard")
    segment, live_rows = layout(seq_lengths, seq_device, device, tokens.shape[0])
    live_float = live_rows.astype(jnp.float32)[:, None]
    in_low = in_weight.astype(jnp.bfloat16)
    kernel_low = conv_kernel.astype(jnp.bfloat16)
    out_low = out_weight.astype(jnp.bfloat16)
    gain_low = norm_gain.astype(jnp.bfloat16)
    gate_low = gate_weight.astype(jnp.bfloat16)
    up_low = up_weight.astype(jnp.bfloat16)
    down_low = down_weight.astype(jnp.bfloat16)
    in_w, kernel_w, out_w, gain_w, gate_w, up_w, down_w = (
        lax.all_gather(in_low, "shard", axis=0, tiled=True),
        lax.all_gather(kernel_low, "shard", axis=0, tiled=True),
        lax.all_gather(out_low, "shard", axis=0, tiled=True),
        lax.all_gather(gain_low, "shard", axis=0, tiled=True),
        lax.all_gather(gate_low, "shard", axis=0, tiled=True),
        lax.all_gather(up_low, "shard", axis=0, tiled=True),
        lax.all_gather(down_low, "shard", axis=0, tiled=True),
    )
    model_width = in_w.shape[0]
    projected = product(tokens, in_w)
    b_branch = projected[:, :model_width]
    c_branch = projected[:, model_width : 2 * model_width]
    x_branch = projected[:, 2 * model_width :]
    mixed = b_branch * x_branch
    kernel_f = kernel_w.astype(jnp.float32)
    convolved, matches = conv_forward(mixed, kernel_f, segment)
    conv_low = (c_branch * convolved).astype(jnp.bfloat16)
    hidden = tokens.astype(jnp.float32) + product(conv_low, out_w)
    inv_rms = lax.rsqrt(jnp.mean(hidden * hidden, axis=-1, keepdims=True) + NORM_EPS)
    gain_f = gain_w.astype(jnp.float32)
    scaled = hidden * inv_rms
    normed = (scaled * gain_f).astype(jnp.bfloat16)
    gate_pre = product(normed, gate_w)
    up_pre = product(normed, up_w)
    sigmoid_gate = jax.nn.sigmoid(gate_pre)
    silu_gate = gate_pre * sigmoid_gate
    act_low = (silu_gate * up_pre).astype(jnp.bfloat16)
    ffn_out = product(act_low, down_w)
    block_out = ((hidden + ffn_out) * live_float).astype(jnp.bfloat16)
    in_b, kernel_b, out_b, gain_b, gate_b, up_b, down_b = (
        lax.all_gather(in_low, "shard", axis=0, tiled=True),
        lax.all_gather(kernel_low, "shard", axis=0, tiled=True),
        lax.all_gather(out_low, "shard", axis=0, tiled=True),
        lax.all_gather(gain_low, "shard", axis=0, tiled=True),
        lax.all_gather(gate_low, "shard", axis=0, tiled=True),
        lax.all_gather(up_low, "shard", axis=0, tiled=True),
        lax.all_gather(down_low, "shard", axis=0, tiled=True),
    )
    grad_out = cotangent.astype(jnp.float32) * live_float
    grad_low = grad_out.astype(jnp.bfloat16)
    grad_act = product_nt(grad_low, down_b)
    grad_down = product_tn(act_low, grad_low)
    grad_upact = (grad_act * silu_gate).astype(jnp.bfloat16)
    grad_gateact = (
        grad_act * up_pre * sigmoid_gate * (1.0 + gate_pre * (1.0 - sigmoid_gate))
    ).astype(jnp.bfloat16)
    grad_norm = product_nt(grad_gateact, gate_b) + product_nt(grad_upact, up_b)
    grad_gate = product_tn(normed, grad_gateact)
    grad_up = product_tn(normed, grad_upact)
    grad_gain = jnp.sum(grad_norm * scaled, axis=0)
    weighted = grad_norm * gain_b.astype(jnp.float32)
    grad_hidden = (
        grad_out
        + inv_rms * weighted
        - scaled * inv_rms * inv_rms * jnp.mean(weighted * hidden, axis=-1, keepdims=True)
    )
    grad_mix = grad_hidden.astype(jnp.bfloat16)
    grad_conv_out = product_nt(grad_mix, out_b)
    grad_out_w = product_tn(conv_low, grad_mix)
    grad_c = grad_conv_out * convolved
    grad_conv = grad_conv_out * c_branch
    grad_mixed, grad_kernel = conv_backward(grad_conv, mixed, kernel_b.astype(jnp.float32), matches)
    grad_proj = jnp.concatenate(
        [grad_mixed * x_branch, grad_c, grad_mixed * b_branch], axis=1
    ).astype(jnp.bfloat16)
    input_grad = grad_hidden + product_nt(grad_proj, in_b)
    grad_in = product_tn(tokens, grad_proj)
    owned_in, owned_kernel, owned_out, owned_gain, owned_gate, owned_up, owned_down = (
        lax.psum_scatter(grad_in, "shard", scatter_dimension=0, tiled=True),
        lax.psum_scatter(grad_kernel, "shard", scatter_dimension=0, tiled=True),
        lax.psum_scatter(grad_out_w, "shard", scatter_dimension=0, tiled=True),
        lax.psum_scatter(grad_gain, "shard", scatter_dimension=0, tiled=True),
        lax.psum_scatter(grad_gate, "shard", scatter_dimension=0, tiled=True),
        lax.psum_scatter(grad_up, "shard", scatter_dimension=0, tiled=True),
        lax.psum_scatter(grad_down, "shard", scatter_dimension=0, tiled=True),
    )
    gradients = lax.psum(
        (owned_in, owned_kernel, owned_out, owned_gain, owned_gate, owned_up, owned_down), "rep"
    )
    bias_one = 1.0 - BETA_ONE**STEP
    bias_two = 1.0 - BETA_TWO**STEP
    updated = []
    firsts = []
    seconds = []
    for master, moment, variance, gradient, step_rate, decay_rate in zip(
        masters, moments, squares, gradients, STEP_RATES, DECAY_RATES
    ):
        first_new = BETA_ONE * moment + (1.0 - BETA_ONE) * gradient
        second_new = BETA_TWO * variance + (1.0 - BETA_TWO) * gradient * gradient
        normalized = first_new / bias_one / (jnp.sqrt(second_new / bias_two) + ADAM_EPS)
        updated.append(master - step_rate * (normalized + decay_rate * master))
        firsts.append(first_new)
        seconds.append(second_new)
    return (
        block_out,
        input_grad,
        updated[0],
        updated[1],
        updated[2],
        updated[3],
        updated[4],
        updated[5],
        updated[6],
        firsts[0],
        firsts[1],
        firsts[2],
        firsts[3],
        firsts[4],
        firsts[5],
        firsts[6],
        seconds[0],
        seconds[1],
        seconds[2],
        seconds[3],
        seconds[4],
        seconds[5],
        seconds[6],
    )


def solution(mesh):
    return jax.shard_map(
        body,
        mesh=mesh,
        in_specs=(
            P(("rep", "shard"), None),
            P(("rep", "shard"), None),
            P(),
            P(),
            P("shard", None),
            P("shard", None),
            P("shard", None),
            P("shard"),
            P("shard", None),
            P("shard", None),
            P("shard", None),
            P("shard", None),
            P("shard", None),
            P("shard", None),
            P("shard"),
            P("shard", None),
            P("shard", None),
            P("shard", None),
            P("shard", None),
            P("shard", None),
            P("shard", None),
            P("shard"),
            P("shard", None),
            P("shard", None),
            P("shard", None),
        ),
        out_specs=(
            P(("rep", "shard"), None),
            P(("rep", "shard"), None),
            P("shard", None),
            P("shard", None),
            P("shard", None),
            P("shard"),
            P("shard", None),
            P("shard", None),
            P("shard", None),
            P("shard", None),
            P("shard", None),
            P("shard", None),
            P("shard"),
            P("shard", None),
            P("shard", None),
            P("shard", None),
            P("shard", None),
            P("shard", None),
            P("shard", None),
            P("shard"),
            P("shard", None),
            P("shard", None),
            P("shard", None),
        ),
        check_vma=False,
    )
```

profile of v0, /device:TPU:1, one launch (start us, length us, event | category | flops | bytes accessed | tf_op | source)
XLA Modules:
  0.0 2483.2 jit_solution(2648038600165985724)
XLA Ops:
  7.2 1.6 convert_element_type.88
  8.9 1.5 convert_element_type.93
  10.4 1.6 convert_element_type.98
  12.1 1.6 convert_element_type.97
  13.9 1.6 convert_element_type.100
  16.2 0.7 select_bitcast_fusion
  18.1 1.3 fusion.37
  20.4 141.0 %all-reduce.6 = bf16[1024]{0:T(1024)(128)(2,1)S(1)} all-reduce(bf16[1024]{0:T(1024)(128)(2,1)S(1)} %dynamic-update-slice), channel_id=1, replica_groups=mesh['rep'=2,'shard'=64] {'shard'}, use_global_device_ids=true, to_apply=%add.6 | all-reduce | flops 1024 | bytes 4096
  162.0 82.1 %all-gather = bf16[64,16,3]{1,2,0:T(4,128)(2,1)S(1)} all-gather(bf16[1,16,3]{1,2,0:T(4,128)(2,1)S(1)} %convert_bitcast_fusion), channel_id=1, replica_groups=mesh['rep'=2,'shard'=64] {'shard'}, dimensions={0}, use_global_device_ids=true | all-gather | bytes 6240 | tf_op jit(solution)/shard_map/all_gather | solution.py:109
  245.4 4.8 fusion.38
  250.4 1.6 copy-done
  252.0 1.4 multiply_convert_fusion.7
  253.4 2.4 multiply_reduce_fusion.5
  256.0 86.4 %all-gather.13.cloned.1.call-done = bf16[1024,4608]{1,0:T(8,128)(2,1)} async-done(((bf16[16,4608]{1,0:T(8,128)(2,1)}), bf16[1024,4608]{1,0:T(8,128)(2,1)}) %all-gather.13.cloned.1.call-update) | async-done | bytes 9437200 | tf_op jit(solution)/shard_map/all_gather | solution.py:113
  342.4 7.9 fusion.40
  350.3 106.3 %all-gather.11.cloned.1.call-done = bf16[1024,4608]{1,0:T(8,128)(2,1)} async-done(((bf16[16,4608]{1,0:T(8,128)(2,1)}), bf16[1024,4608]{1,0:T(8,128)(2,1)}) %all-gather.11.cloned.1.call-update) | async-done | bytes 9437200 | tf_op jit(solution)/shard_map/all_gather | solution.py:112
  456.6 7.9 fusion.39
  464.6 106.5 %all-gather.15.cloned.1.call-done = bf16[4608,1024]{1,0:T(8,128)(2,1)} async-done(((bf16[72,1024]{1,0:T(8,128)(2,1)}), bf16[4608,1024]{1,0:T(8,128)(2,1)}) %all-gather.15.cloned.1.call-update) | async-done | bytes 9437200 | tf_op jit(solution)/shard_map/all_gather | solution.py:114
  571.0 10.0 multiply_convert_fusion
  581.1 2.6 fusion.41
  583.7 5.5 multiply_reduce_fusion
  589.7 1.0 copy-done.3
  590.7 2.8 fusion.11
  593.8 3.8 multiply_reduce_fusion.3
  598.7 6.4 convolution_bitcast_fusion
  605.0 12.6 copy.94
  617.7 1.0 copy-done.11
  618.7 9.6 fusion.15
  628.4 9.7 fusion.43
  638.1 9.6 fusion.42
  647.8 1.1 copy.96
  649.6 227.6 %reduce-scatter.11.cloned.1.call-done = f32[16,1024]{1,0:T(8,128)} async-done(((f32[1024,1024]{1,0:T(8,128)}), f32[16,1024]{1,0:T(8,128)}) %reduce-scatter.11.cloned.1.call-update) | async-done | bytes 65552 | tf_op jit(solution)/shard_map/reduce_scatter | solution.py:178
  877.2 305.2 %reduce-scatter.19.cloned.1.call-done = f32[16,3072]{1,0:T(8,128)} async-done(((f32[1024,3072]{1,0:T(8,128)}), f32[16,3072]{1,0:T(8,128)}) %reduce-scatter.19.cloned.1.call-update) | async-done | bytes 196624 | tf_op jit(solution)/shard_map/reduce_scatter | solution.py:176
  1182.4 316.1 %reduce-scatter.17.cloned.1.call-done = f32[72,1024]{1,0:T(8,128)} async-done(((f32[4608,1024]{1,0:T(8,128)}), f32[72,1024]{1,0:T(8,128)}) %reduce-scatter.17.cloned.1.call-update) | async-done | bytes 294928 | tf_op jit(solution)/shard_map/reduce_scatter | solution.py:182
  1498.5 316.1 %reduce-scatter.15.cloned.1.call-done = f32[16,4608]{1,0:T(8,128)} async-done(((f32[1024,4608]{1,0:T(8,128)}), f32[16,4608]{1,0:T(8,128)}) %reduce-scatter.15.cloned.1.call-update) | async-done | bytes 294928 | tf_op jit(solution)/shard_map/reduce_scatter | solution.py:181
  1814.6 316.4 %reduce-scatter.13.cloned.1.call-done = f32[16,4608]{1,0:T(8,128)} async-done(((f32[1024,4608]{1,0:T(8,128)}), f32[16,4608]{1,0:T(8,128)}) %reduce-scatter.13.cloned.1.call-update) | async-done | bytes 294928 | tf_op jit(solution)/shard_map/reduce_scatter | solution.py:180
  2131.0 7.9 fusion.2
  2138.9 144.4 %all-reduce.7 = f32[1024]{0:T(1024)S(1)} all-reduce(f32[1024]{0:T(1024)S(1)} %get-tuple-element.115), channel_id=5, replica_groups=mesh['rep'=2,'shard'=64] {'shard'}, use_global_device_ids=true, to_apply=%region_15.16.clone | all-reduce | flops 1024 | bytes 8192
  2284.0 5.9 convolution_add_fusion.3
  2289.9 124.5 %reduce-scatter.21.cloned.1.call-done = f32[16,3]{1,0:T(8,128)} async-done(((f32[1024,3]{1,0:T(8,128)}), f32[16,3]{1,0:T(8,128)}) %reduce-scatter.21.cloned.1.call-update) | async-done | bytes 208
  2414.4 0.8 copy.97
  2415.1 5.4 all-reduce.8
  2420.5 1.2 multiply_subtract_fusion.7
  2422.4 46.7 %all-reduce.12.cloned.1.call-done = (f32[16,3072]{1,0:T(8,128)}, f32[16,1024]{1,0:T(8,128)}, f32[16,4608]{1,0:T(8,128)}, f32[16,4608]{1,0:T(8,128)}, f32[72,1024]{1,0:T(8,128)}) async-done(((f32[16,3072]{1,0:T(8,128)}, f32[16,1024]{1,0:T(8,128)}, f32[16,4608]{1,0:T(8,128)}, f32[16,4608]{1,0:T(8,128)}, f32[72,1024]{1,0:T(8,128)}), (f32[16,3072]{1,0:T(8,128)}, f32[16,1024]{1,0:T(8,128)}, ...) | async-done | bytes 1146896 | tf_op jit(solution)/shard_map/psum | solution.py:184
  2469.0 1.6 multiply_subtract_fusion.5
  2470.6 2.0 multiply_subtract_fusion.4
  2472.6 2.2 multiply_subtract_fusion.1
  2474.9 1.5 multiply_subtract_fusion.2
  (109 shorter events, 8.0 us)
Async XLA Ops:
  7.2 238.2 %all-gather.7.cloned.1.call-start = ((), (), s32[]{:S(2)}) async-start(), calls=%async_computation.6 | async-start | bytes 6389760 | tf_op jit(solution)/shard_map/all_gather | solution.py:108
  8.8 244.6 %all-gather.9.cloned.1.call-start = ((), (), s32[]{:S(2)}) async-start(), calls=%async_computation.7 | async-start | bytes 2129920 | tf_op jit(solution)/shard_map/all_gather | solution.py:110
  10.4 332.1 %all-gather.13.cloned.1.call-start = ((), (), s32[]{:S(2)}) async-start(), calls=%async_computation.9 | async-start | bytes 9584640 | tf_op jit(solution)/shard_map/all_gather | solution.py:113
  12.1 444.5 %all-gather.11.cloned.1.call-start = ((), (), s32[]{:S(2)}) async-start(), calls=%async_computation.8 | async-start | bytes 9584640 | tf_op jit(solution)/shard_map/all_gather | solution.py:112
  13.8 557.2 %all-gather.15.cloned.1.call-start = ((), (), s32[]{:S(2)}) async-start(), calls=%async_computation.10 | async-start | bytes 9584640 | tf_op jit(solution)/shard_map/all_gather | solution.py:114
  15.5 861.6 %reduce-scatter.11.cloned.1.call-start = ((), (), s32[]{:S(2)}) async-start(), calls=%async_computation.11 | async-start | bytes 4259840 | tf_op jit(solution)/shard_map/reduce_scatter | solution.py:178
  250.2 1.7 copy-start
  250.2 3.2 copy-start.7
  571.0 10.0 copy-start.2
  581.1 2.6 copy-start.5
  581.1 2.6 copy-start.6
  583.7 5.6 copy-start.10
  589.7 1.0 copy-start.3
  593.5 588.9 %reduce-scatter.19.cloned.1.call-start = ((), (), s32[]{:S(2)}) async-start(), calls=%async_computation.15 | async-start | bytes 12779520 | tf_op jit(solution)/shard_map/reduce_scatter | solution.py:176
  593.8 3.8 copy-start.1
  597.6 1.0 copy-start.8
  598.3 6.7 copy-start.9
  617.7 1.0 copy-start.11
  617.7 880.9 %reduce-scatter.17.cloned.1.call-start = ((), (), s32[]{:S(2)}) async-start(), calls=%async_computation.14 | async-start | bytes 19169280 | tf_op jit(solution)/shard_map/reduce_scatter | solution.py:182
  628.3 1186.3 %reduce-scatter.15.cloned.1.call-start = ((), (), s32[]{:S(2)}) async-start(), calls=%async_computation.13 | async-start | bytes 19169280 | tf_op jit(solution)/shard_map/reduce_scatter | solution.py:181
  638.1 1492.9 %reduce-scatter.13.cloned.1.call-start = ((), (), s32[]{:S(2)}) async-start(), calls=%async_computation.12 | async-start | bytes 19169280 | tf_op jit(solution)/shard_map/reduce_scatter | solution.py:180
  647.7 1766.7 %reduce-scatter.21.cloned.1.call-start = ((), (), s32[]{:S(2)}) async-start(), calls=%async_computation.16 | async-start | bytes 532480
  648.9 1820.1 %all-reduce.12.cloned.1.call-start = ((), (), s32[]{:S(2)}) async-start(), calls=%async_computation.17 | async-start | bytes 2293760 | tf_op jit(solution)/shard_map/psum | solution.py:184
  2131.0 152.9 %copy-start.4 = (f32[256,1024]{1,0:T(8,128)S(1)}, f32[256,1024]{1,0:T(8,128)}, u32[]{:S(2)}) copy-start(f32[256,1024]{1,0:T(8,128)} %copy-done.3) | copy-start | bytes 3145732
  2283.9 136.6 %copy-start.28 = (f32[16]{0:T(128)S(1)}, f32[16]{0:T(128)}, u32[]{:S(2)}) copy-start(f32[16]{0:T(128)} %param.32) | copy-start | bytes 196
  2283.9 137.8 %copy-start.25 = (f32[16,3]{0,1:T(4,128)S(1)}, f32[16,3]{0,1:T(4,128)}, u32[]{:S(2)}) copy-start(f32[16,3]{0,1:T(4,128)} %param.30) | copy-start | bytes 580
  2283.9 137.8 %copy-start.26 = (f32[16,3]{0,1:T(4,128)S(1)}, f32[16,3]{0,1:T(4,128)}, u32[]{:S(2)}) copy-start(f32[16,3]{0,1:T(4,128)} %param.37) | copy-start | bytes 580
  2283.9 137.8 %copy-start.27 = (f32[16,3]{0,1:T(4,128)S(1)}, f32[16,3]{0,1:T(4,128)}, u32[]{:S(2)}) copy-start(f32[16,3]{0,1:T(4,128)} %param.44) | copy-start | bytes 580
  2283.9 185.1 %copy-start.22 = (f32[16,1024]{1,0:T(8,128)S(1)}, f32[16,1024]{1,0:T(8,128)}, u32[]{:S(2)}) copy-start(f32[16,1024]{1,0:T(8,128)} %param.31) | copy-start | bytes 196612
  2283.9 185.1 %copy-start.23 = (f32[16,1024]{1,0:T(8,128)S(1)}, f32[16,1024]{1,0:T(8,128)}, u32[]{:S(2)}) copy-start(f32[16,1024]{1,0:T(8,128)} %param.38) | copy-start | bytes 196612
  2283.9 185.1 %copy-start.24 = (f32[16,1024]{1,0:T(8,128)S(1)}, f32[16,1024]{1,0:T(8,128)}, u32[]{:S(2)}) copy-start(f32[16,1024]{1,0:T(8,128)} %param.45) | copy-start | bytes 196612
  2284.0 186.7 %copy-start.15 = (f32[16,3072]{1,0:T(8,128)S(1)}, f32[16,3072]{1,0:T(8,128)}, u32[]{:S(2)}) copy-start(f32[16,3072]{1,0:T(8,128)} %param.29) | copy-start | bytes 589828
  2284.0 188.7 %copy-start.14 = (f32[72,1024]{1,0:T(8,128)S(1)}, f32[72,1024]{1,0:T(8,128)}, u32[]{:S(2)}) copy-start(f32[72,1024]{1,0:T(8,128)} %param.35) | copy-start | bytes 884740
  2289.9 185.0 %copy-start.12 = (f32[16,4608]{1,0:T(8,128)S(1)}, f32[16,4608]{1,0:T(8,128)}, u32[]{:S(2)}) copy-start(f32[16,4608]{1,0:T(8,128)} %param.34) | copy-start | bytes 884740
  2289.9 185.0 %copy-start.13 = (f32[16,4608]{1,0:T(8,128)S(1)}, f32[16,4608]{1,0:T(8,128)}, u32[]{:S(2)}) copy-start(f32[16,4608]{1,0:T(8,128)} %param.33) | copy-start | bytes 884740
  2289.9 185.0 %copy-start.16 = (f32[16,4608]{1,0:T(8,128)S(1)}, f32[16,4608]{1,0:T(8,128)}, u32[]{:S(2)}) copy-start(f32[16,4608]{1,0:T(8,128)} %param.41) | copy-start | bytes 884740
  2289.9 185.0 %copy-start.17 = (f32[16,4608]{1,0:T(8,128)S(1)}, f32[16,4608]{1,0:T(8,128)}, u32[]{:S(2)}) copy-start(f32[16,4608]{1,0:T(8,128)} %param.48) | copy-start | bytes 884740
  2289.9 185.0 %copy-start.18 = (f32[16,4608]{1,0:T(8,128)S(1)}, f32[16,4608]{1,0:T(8,128)}, u32[]{:S(2)}) copy-start(f32[16,4608]{1,0:T(8,128)} %param.47) | copy-start | bytes 884740
  2289.9 185.0 %copy-start.19 = (f32[16,4608]{1,0:T(8,128)S(1)}, f32[16,4608]{1,0:T(8,128)}, u32[]{:S(2)}) copy-start(f32[16,4608]{1,0:T(8,128)} %param.40) | copy-start | bytes 884740
  2469.0 5.9 copy-start.20
  2469.0 5.9 copy-start.21
Sparse Core Ops, SparseCore 0:
  10.3 112.4 all-gather.6
  125.1 102.3 all-gather.8
  229.8 112.5 all-gather.12
  344.6 111.9 all-gather.10
  458.8 112.2 all-gather.14
  593.6 283.4 reduce-scatter.10
  879.7 302.6 reduce-scatter.18
  1185.0 313.5 reduce-scatter.16
  1501.1 313.4 reduce-scatter.14
  1817.0 313.8 reduce-scatter.12
  2133.4 280.8 reduce-scatter.20
  2417.0 51.9 all-reduce.11
where the time goes:
time: 2480 us
  waiting for transfers between devices  1950 us (79%)
  blocking collectives  373 us (15%)
  matrix products  96.8 us (4%)
    reduce_scatter x1, waiting for transfers between devices, body(): lax.psum_scatter(grad_gate, 'shard', scatter_dimension=0, tiled=True)  316 us
    reduce_scatter x1, waiting for transfers between devices, body(): lax.psum_scatter(grad_down, 'shard', scatter_dimension=0, tiled=True)  316 us
    reduce_scatter x1, waiting for transfers between devices, body(): lax.psum_scatter(grad_up, 'shard', scatter_dimension=0, tiled=True)  316 us
    reduce_scatter x1, waiting for transfers between devices, body(): lax.psum_scatter(grad_in, 'shard', scatter_dimension=0, tiled=True)  305 us
    unnamed x2, blocking collectives  285 us
    reduce_scatter x1, waiting for transfers between devices, body(): lax.psum_scatter(grad_out_w, 'shard', scatter_dimension=0, tiled=True)  228 us
    unnamed x13, waiting for transfers between devices  125 us
    all_gather x1, waiting for transfers between devices, body(): lax.all_gather(down_low, 'shard', axis=0, tiled=True)  106 us
  transfers between devices with their start and end apart: 12, of which 10 were waited for; matrix products, arithmetic and copies ran while one was open for 4% of the time, Pallas kernels for 0%

commit v1 on v0

v1 whole, which is shorter than its diff:
```python
import jax
import jax.numpy as jnp
from jax import lax
from jax.experimental import pallas as pl
from jax.experimental.pallas import tpu as pltpu
from jax.sharding import Mesh
from jax.sharding import PartitionSpec as P

STEP = 10
NORM_EPS = 1e-05
BETA_ONE = 0.9
BETA_TWO = 0.95
ADAM_EPS = 1e-08
STEP_RATES = (0.02, 0.3, 0.02, 0.3, 0.02, 0.02, 0.02)
DECAY_RATES = (0.1, 0.0, 0.1, 0.0, 0.1, 0.1, 0.1)

AXES = ("rep", "z", "x", "y", "core")
SHARD = ("z", "x", "y", "core")
SIDE = 4
AUX = 128


def layout(seq_lengths, seq_device, device, row_count):
    owned_len = jnp.where(seq_device == device, seq_lengths, 0)
    seq_ends = jnp.cumsum(owned_len, dtype=jnp.int32)
    slot_index = jnp.arange(row_count, dtype=jnp.int32)
    segment = jnp.sum(
        (seq_ends[None, :] <= slot_index[:, None]).astype(jnp.int32), axis=1, dtype=jnp.int32
    )
    live_rows = (slot_index < seq_ends[-1]).astype(jnp.int32)
    return (segment, live_rows)


def product(left, right):
    return jnp.dot(left, right, preferred_element_type=jnp.float32)


def product_nt(left, right):
    return lax.dot_general(
        left, right, (((1,), (1,)), ((), ())), preferred_element_type=jnp.float32
    )


def product_tn(left, right):
    return lax.dot_general(
        left, right, (((0,), (0,)), ((), ())), preferred_element_type=jnp.float32
    )


def conv_forward(mixed, taps, segment):
    summed = mixed * taps[0]
    matches = []
    for offset in range(1, len(taps)):
        earlier = jnp.pad(mixed, ((offset, 0), (0, 0)))[:-offset]
        same_seq = (jnp.pad(segment, (offset, 0), constant_values=-1)[:-offset] == segment)[:, None]
        matches.append(same_seq)
        summed = summed + jnp.where(same_seq, earlier * taps[offset], 0.0)
    return (summed, matches)


def conv_backward(gradient, mixed, taps, matches):
    grad_mixed = gradient * taps[0]
    grad_taps = [jnp.sum(gradient * mixed, axis=0)]
    for offset in range(1, len(taps)):
        masked = jnp.where(matches[offset - 1], gradient, 0.0)
        later = jnp.pad(masked, ((0, offset), (0, 0)))[offset:]
        grad_mixed = grad_mixed + later * taps[offset]
        earlier = jnp.pad(mixed, ((offset, 0), (0, 0)))[:-offset]
        grad_taps.append(jnp.sum(masked * earlier, axis=0))
    return (grad_mixed, grad_taps)


def low(value):
    return value.astype(jnp.bfloat16)


def wide(value):
    return value.astype(jnp.float32)


def after(value, *earlier):
    return lax.optimization_barrier((value,) + earlier)[0]


def plane_shift(value, distance, turn):
    pairs = []
    for z in range(SIDE):
        for x in range(SIDE):
            for core in range(2):
                if (core + turn) % 2 == 0:
                    to_z, to_x = z, (x + distance) % SIDE
                else:
                    to_z, to_x = (z + distance) % SIDE, x
                pairs.append(((z * SIDE + x) * 2 + core, (to_z * SIDE + to_x) * 2 + core))
    return lax.ppermute(value, ("z", "x", "core"), pairs)


def ring_shift(value, distance, swap=0):
    pairs = []
    for y in range(SIDE):
        for core in range(2):
            pairs.append((y * 2 + core, (y + distance) % SIDE * 2 + (core + swap) % 2))
    return lax.ppermute(value, ("rep", "y", "core"), pairs)


def core_swap(value):
    return lax.ppermute(value, "core", [(0, 1), (1, 0)])


def pair_swap(value):
    return lax.ppermute(value, "y", [(0, 1), (1, 0)])


def in_order(index, mine, other):
    first = jnp.where(index == 0, mine, other)
    second = jnp.where(index == 0, other, mine)
    return jnp.concatenate([first, second], axis=0)


def any_specs(count):
    return [pl.BlockSpec(memory_space=pl.ANY)] * count


def move_blocks(sources, out_shapes, index, moves):
    count = len(sources)

    def kernel(index_ref, *refs):
        sems = refs[-1]
        ins, outs = refs[:count], refs[count:-1]
        copies = [
            pltpu.make_async_copy(source, target, sems.at[i])
            for i, (source, target) in enumerate(moves(ins, outs, index_ref))
        ]
        for copy in copies:
            copy.start()
        for copy in copies:
            copy.wait()

    total = sum(1 for _ in moves_count(moves, sources, out_shapes))
    moved = sum(s.size * s.dtype.itemsize for s in out_shapes)
    return pl.pallas_call(
        kernel,
        out_shape=out_shapes,
        in_specs=[pl.BlockSpec(memory_space=pltpu.SMEM)] + any_specs(count),
        out_specs=any_specs(len(out_shapes)),
        scratch_shapes=[pltpu.SemaphoreType.DMA((total,))],
        cost_estimate=pl.CostEstimate(flops=0, bytes_accessed=2 * moved, transcendentals=0),
    )(index, *sources)


class Blank:
    @property
    def at(self):
        return self

    def __getitem__(self, key):
        return self


def moves_count(moves, sources, out_shapes):
    class Index:
        def __getitem__(self, key):
            return 0

    return list(moves([Blank()] * len(sources), [Blank()] * len(out_shapes), Index()))


def gather_plane(block):
    first = [block] + [plane_shift(block, d, 0) for d in (1, 2, 3)]
    joined = jnp.concatenate(first, axis=0)
    return [joined] + [plane_shift(joined, d, 1) for d in (1, 2, 3)]


def plane_places(z, x, core):
    places = []
    for d2 in range(SIDE):
        for d1 in range(SIDE):
            at_z = jnp.where(core == 0, (z - d2) % SIDE, (z - d1) % SIDE)
            at_x = jnp.where(core == 0, (x - d1) % SIDE, (x - d2) % SIDE)
            places.append(at_z * SIDE + at_x)
    return jnp.stack(places).astype(jnp.int32)


def plane_sources(z, x, core):
    picks = []
    for d in range(SIDE):
        for k in range(SIDE):
            at_z = jnp.where(core == 0, (z + d) % SIDE, k)
            at_x = jnp.where(core == 0, k, (x + d) % SIDE)
            picks.append(at_z * SIDE + at_x)
    return jnp.stack(picks).astype(jnp.int32)


def sum_wide(parts):
    total = wide(parts[0])
    for part in parts[1:]:
        total = total + wide(part)
    return total


def reduce_plane(blocks, z, x, core):
    rows, columns = blocks.shape[1:]
    shape = jax.ShapeDtypeStruct((SIDE, rows, columns), blocks.dtype)

    def moves(ins, outs, index):
        for d in range(SIDE):
            for k in range(SIDE):
                yield ins[0].at[index[d * SIDE + k]], outs[d].at[k]

    messages = move_blocks([blocks], [shape] * SIDE, plane_sources(z, x, core), moves)
    parts = [messages[0]] + [plane_shift(messages[d], d, 1) for d in (1, 2, 3)]
    summed = low(sum_wide(parts))
    me = jnp.where(core == 0, x, z)
    pick = lambda d: lax.dynamic_index_in_dim(summed, (me + d) % SIDE, 0, keepdims=False)
    return low(sum_wide([pick(0)] + [plane_shift(pick(d), d, 0) for d in (1, 2, 3)]))


def reduce_ring(pair, y):
    own = lax.dynamic_index_in_dim(pair, y, 0, keepdims=False)
    other = lax.dynamic_index_in_dim(pair, 1 - y, 0, keepdims=False)
    return sum_wide([own, ring_shift(other, 1), ring_shift(other, 3), ring_shift(own, 2)])


def body(
    tokens,
    cotangent,
    seq_lengths,
    seq_device,
    in_weight,
    conv_kernel,
    out_weight,
    norm_gain,
    gate_weight,
    up_weight,
    down_weight,
    moment_in,
    moment_conv,
    moment_out,
    moment_gain,
    moment_gate,
    moment_up,
    moment_down,
    square_in,
    square_conv,
    square_out,
    square_gain,
    square_gate,
    square_up,
    square_down,
):
    masters = (in_weight, conv_kernel, out_weight, norm_gain, gate_weight, up_weight, down_weight)
    moments = (moment_in, moment_conv, moment_out, moment_gain, moment_gate, moment_up, moment_down)
    squares = (square_in, square_conv, square_out, square_gain, square_gate, square_up, square_down)
    rep, z, x, y, core = [lax.axis_index(name) for name in AXES]
    device = (((rep * SIDE + z) * SIDE + x) * 2 + y) * 2 + core
    slots, width = tokens.shape
    rows = in_weight.shape[0]
    hidden_units = gate_weight.shape[1]
    half = hidden_units // 2
    down_rows = down_weight.shape[0]
    chips = SIDE * SIDE
    tap_count = conv_kernel.shape[1]
    in_columns = in_weight.shape[1]
    mix_columns = in_columns + width + AUX

    segment, live_rows = layout(seq_lengths, seq_device, device, slots)
    live_float = wide(live_rows)[:, None]
    places = plane_places(z, x, core)

    small = jnp.concatenate([conv_kernel, norm_gain[:, None]], axis=1)
    small = jnp.pad(low(small), ((0, 0), (0, AUX - tap_count - 1)))
    mix_local = jnp.concatenate([low(in_weight), low(out_weight), small], axis=1)
    mix_pair = in_order(y, mix_local, pair_swap(mix_local))
    mix_first = [mix_pair] + [plane_shift(mix_pair, d, 0) for d in (1, 2, 3)]
    mix_joined = jnp.concatenate(mix_first, axis=0)
    mix_own = [mix_joined] + [plane_shift(mix_joined, d, 1) for d in (1, 2, 3)]
    mix_other = [core_swap(part) for part in mix_own]
    other_places = plane_places(z, x, 1 - core)
    parts = [part.reshape(SIDE, 2, rows, mix_columns) for part in mix_own + mix_other]

    def mix_moves(ins, outs, index):
        bounds = [(0, in_columns), (in_columns, width), (in_columns + width, AUX)]
        for side in range(2):
            where = index[2 * chips + side]
            for d2 in range(SIDE):
                for d1 in range(SIDE):
                    place = index[side * chips + d2 * SIDE + d1]
                    for out, (start, size) in zip(outs, bounds):
                        source = ins[side * SIDE + d2].at[d1, :, :, pl.ds(start, size)]
                        yield source, out.at[place, :, where]

    both = jnp.stack([core, 1 - core]).astype(jnp.int32)
    mix_index = jnp.concatenate([places, other_places, both])
    in_w, out_w, small_w = move_blocks(
        parts,
        [
            jax.ShapeDtypeStruct((chips, 2, 2, rows, columns), jnp.bfloat16)
            for columns in (in_columns, width, AUX)
        ],
        mix_index,
        mix_moves,
    )
    in_w = in_w.reshape(width, in_columns)
    out_w = out_w.reshape(width, width)
    small_w = wide(small_w.reshape(width, AUX)[:, : tap_count + 1]).T
    taps = [small_w[k] for k in range(tap_count)]
    gain = small_w[tap_count]

    def by_core(weight):
        return low(weight).reshape(rows, -1, 2, down_rows)

    gate_split, up_split = by_core(gate_weight), by_core(up_weight)
    unit_halves = [
        jnp.concatenate(
            [gate_split[:, :, c].reshape(rows, half), up_split[:, :, c].reshape(rows, half)], axis=1
        )
        for c in range(2)
    ]
    mine = jnp.where(core == 0, unit_halves[0], unit_halves[1])
    theirs = jnp.where(core == 0, unit_halves[1], unit_halves[0])
    unit_pair = in_order(core, mine, core_swap(theirs))
    unit_pair = after(unit_pair, *mix_first)
    unit_first = [unit_pair] + [plane_shift(unit_pair, d, 0) for d in (1, 2, 3)]
    unit_joined = after(jnp.concatenate(unit_first, axis=0), *mix_own)
    unit_own = [unit_joined] + [plane_shift(unit_joined, d, 1) for d in (1, 2, 3)]
    unit_other = [ring_shift(part, 1 if i < 2 else 3) for i, part in enumerate(unit_own)]
    parts = [part.reshape(SIDE, 2 * rows, 2 * half) for part in unit_own + unit_other]

    def unit_moves(ins, outs, index):
        for side in range(2):
            where = index[chips + side]
            for d2 in range(SIDE):
                for d1 in range(SIDE):
                    place = index[d2 * SIDE + d1]
                    yield ins[side * SIDE + d2].at[d1], outs[0].at[place, where]

    unit_index = jnp.concatenate([places, jnp.stack([y, 1 - y]).astype(jnp.int32)])
    (unit_w,) = move_blocks(
        parts,
        [jax.ShapeDtypeStruct((chips, 2, 2 * rows, 2 * half), jnp.bfloat16)],
        unit_index,
        unit_moves,
    )
    unit_w = unit_w.reshape(width, 2 * half)

    down_low = low(down_weight)
    down_pair = in_order(y, down_low, pair_swap(down_low))
    down_pair = after(down_pair, *unit_first)
    down_first = [down_pair] + [plane_shift(down_pair, d, 0) for d in (1, 2, 3)]
    down_joined = after(jnp.concatenate(down_first, axis=0), *unit_own)
    down_own = [down_joined] + [plane_shift(down_joined, d, 1) for d in (1, 2, 3)]
    parts = [part.reshape(SIDE, 2 * down_rows, width) for part in down_own]

    def down_moves(ins, outs, index):
        for d2 in range(SIDE):
            for d1 in range(SIDE):
                yield ins[d2].at[d1], outs[0].at[index[d2 * SIDE + d1]]

    (down_w,) = move_blocks(
        parts,
        [jax.ShapeDtypeStruct((chips, 2 * down_rows, width), jnp.bfloat16)],
        places,
        down_moves,
    )
    down_w = down_w.reshape(half, width)

    projected = product(tokens, in_w)
    b_branch = projected[:, :width]
    c_branch = projected[:, width : 2 * width]
    x_branch = projected[:, 2 * width :]
    mixed = b_branch * x_branch
    convolved, matches = conv_forward(mixed, taps, segment)
    conv_low = low(c_branch * convolved)
    hidden = wide(tokens) + product(conv_low, out_w)
    inv_rms = lax.rsqrt(jnp.mean(hidden * hidden, axis=-1, keepdims=True) + NORM_EPS)
    scaled = hidden * inv_rms
    normed = low(scaled * gain)

    grad_out = wide(cotangent) * live_float
    grad_low = low(grad_out)
    grad_both = jnp.concatenate([grad_low, core_swap(grad_low)], axis=0)
    normed_both = jnp.concatenate([normed, core_swap(normed)], axis=0)
    pre = product(normed_both, unit_w)
    gate_pre, up_pre = pre[:, :half], pre[:, half:]
    sigmoid_gate = jax.nn.sigmoid(gate_pre)
    silu_gate = gate_pre * sigmoid_gate
    act_low = low(silu_gate * up_pre)
    ffn_part = product(act_low, down_w)
    grad_act = product_nt(grad_both, down_w)
    grad_down = low(product_tn(act_low, grad_both))
    grad_up = low(grad_act * silu_gate)
    grad_gate = low(grad_act * up_pre * sigmoid_gate * (1.0 + gate_pre * (1.0 - sigmoid_gate)))
    grad_pre = jnp.concatenate([grad_gate, grad_up], axis=1)
    norm_part = product_nt(grad_pre, unit_w)
    grad_norm = norm_part[:slots] + wide(core_swap(low(norm_part[slots:])))
    ffn_out = ffn_part[:slots] + wide(core_swap(low(ffn_part[slots:])))
    block_out = low((hidden + ffn_out) * live_float)
    grad_unit = low(product_tn(normed_both, grad_pre)).reshape(chips, 2, 2 * rows, 2 * half)

    grad_gain = jnp.sum(grad_norm * scaled, axis=0)
    weighted = grad_norm * gain
    grad_hidden = (
        grad_out
        + inv_rms * weighted
        - scaled * inv_rms * inv_rms * jnp.mean(weighted * hidden, axis=-1, keepdims=True)
    )
    grad_mix = low(grad_hidden)
    grad_conv_out = product_nt(grad_mix, out_w)
    grad_out_w = low(product_tn(conv_low, grad_mix))
    grad_c = grad_conv_out * convolved
    grad_conv = grad_conv_out * c_branch
    grad_mixed, grad_taps = conv_backward(grad_conv, mixed, taps, matches)
    grad_proj = low(jnp.concatenate([grad_mixed * x_branch, grad_c, grad_mixed * b_branch], axis=1))
    input_grad = grad_hidden + product_nt(grad_proj, in_w)
    grad_in = low(product_tn(tokens, grad_proj))

    down_sum = reduce_plane(grad_down.reshape(chips, 2 * down_rows, width), z, x, core)
    total_down = reduce_ring(down_sum.reshape(2, down_rows, width), y)

    other_rows = lax.dynamic_index_in_dim(grad_unit, 1 - y, 1, keepdims=False)
    own_rows = lax.dynamic_index_in_dim(grad_unit, y, 1, keepdims=False)
    from_gate = ring_shift(other_rows[:, :, :half], 1)
    from_up = ring_shift(other_rows[:, :, half:], 3)
    unit_rows = jnp.concatenate(
        [
            low(wide(own_rows[:, :, :half]) + wide(from_gate)),
            low(wide(own_rows[:, :, half:]) + wide(from_up)),
        ],
        axis=2,
    )
    unit_sum = reduce_plane(unit_rows, z, x, core).reshape(2, rows, 2 * half)
    own = lax.dynamic_index_in_dim(unit_sum, core, 0, keepdims=False)
    other = lax.dynamic_index_in_dim(unit_sum, 1 - core, 0, keepdims=False)
    own_units = wide(own) + wide(ring_shift(own, 2))
    other_units = wide(ring_shift(other, 0, 1)) + wide(ring_shift(other, 2, 1))
    unit_zero = jnp.where(core == 0, own_units, other_units)
    unit_one = jnp.where(core == 0, other_units, own_units)

    def merge(first, second):
        pair = [part.reshape(rows, -1, down_rows) for part in (first, second)]
        return jnp.stack(pair, axis=2).reshape(rows, hidden_units)

    total_gate = merge(unit_zero[:, :half], unit_one[:, :half])
    total_up = merge(unit_zero[:, half:], unit_one[:, half:])

    grad_small = jnp.stack(grad_taps + [grad_gain], axis=1)
    grad_small = jnp.pad(low(grad_small), ((0, 0), (0, AUX - tap_count - 1)))
    mix_blocks = [
        part.reshape(chips, 2, 2, rows, -1) for part in (grad_in, grad_out_w, grad_small)
    ]

    def of_core(which):
        picked = [lax.dynamic_index_in_dim(part, which, 2, keepdims=False) for part in mix_blocks]
        return jnp.concatenate(picked, axis=-1).reshape(chips, 2 * rows, mix_columns)

    mix_rows = low(wide(of_core(core)) + wide(core_swap(of_core(1 - core))))
    mix_sum = reduce_plane(mix_rows, z, x, core)
    total_mix = reduce_ring(mix_sum.reshape(2, rows, mix_columns), y)
    total_small = total_mix[:, in_columns + width :]
    gradients = (
        total_mix[:, :in_columns],
        total_small[:, :tap_count],
        total_mix[:, in_columns : in_columns + width],
        total_small[:, tap_count],
        total_gate,
        total_up,
        total_down,
    )
    bias_one = 1.0 - BETA_ONE**STEP
    bias_two = 1.0 - BETA_TWO**STEP
    updated = []
    firsts = []
    seconds = []
    for master, moment, variance, gradient, step_rate, decay_rate in zip(
        masters, moments, squares, gradients, STEP_RATES, DECAY_RATES
    ):
        first_new = BETA_ONE * moment + (1.0 - BETA_ONE) * gradient
        second_new = BETA_TWO * variance + (1.0 - BETA_TWO) * gradient * gradient
        normalized = first_new / bias_one / (jnp.sqrt(second_new / bias_two) + ADAM_EPS)
        updated.append(master - step_rate * (normalized + decay_rate * master))
        firsts.append(first_new)
        seconds.append(second_new)
    return (block_out, input_grad, *updated, *firsts, *seconds)


def solution(mesh):
    grid = Mesh(mesh.devices.reshape(2, SIDE, SIDE, 2, 2), AXES)
    by_token = P(AXES, None)
    matrix, vector = P(SHARD, None), P(SHARD)
    group = (matrix, matrix, matrix, vector, matrix, matrix, matrix)
    return jax.shard_map(
        body,
        mesh=grid,
        in_specs=(by_token, by_token, P(), P(), *group, *group, *group),
        out_specs=(by_token, by_token, *group, *group, *group),
        check_vma=False,
    )
```

time: 2480 us -> 1550 us (0.62)
  waiting for transfers between devices: 1950 us -> 130 us
  Pallas kernels: 0 us -> 1120 us
  blocking collectives: 373 us -> 0 us
  starting transfers between devices: 0.72 us -> 100 us
  local copies, waits for them, and re-layouts: 21.6 us -> 67.3 us
  matrix products: 96.8 us -> 60.2 us
  other arithmetic: 23.2 us -> 51.9 us
    reduce_scatter x5 -> x0, waiting for transfers between devices: 1480 us -> none  [the longest x1 316 us: body(): lax.psum_scatter(grad_gate, 'shard', scatter_dimension=0, tiled=True)]
    pallas_call x0 -> x6, Pallas kernels: none -> 1120 us  [move_blocks(): pl.pallas_call(kernel, out_shape=out_shapes, in_specs=[pl.BlockSpec(memor...]
    all_gather x5 -> x0, waiting for transfers between devices: 299 us -> none  [the longest x1 106 us: body(): lax.all_gather(down_low, 'shard', axis=0, tiled=True)]
    unnamed x2 -> x0, blocking collectives: 285 us -> none
    ppermute x0 -> x63, waiting for transfers between devices: none -> 130 us  [the longest x36 91.6 us: plane_shift(): return lax.ppermute(value, ('z', 'x', 'core'), pairs)]
    unnamed x13 -> x0, waiting for transfers between devices: 125 us -> none
    ppermute x0 -> x63, starting transfers between devices: none -> 100 us  [the longest x36 50.9 us: plane_shift(): return lax.ppermute(value, ('z', 'x', 'core'), pairs)]
    all_gather x1 -> x0, blocking collectives: 82.1 us -> none  [body(): lax.all_gather(kernel_low, 'shard', axis=0, tiled=True)]
  transfers between devices with their start and end apart: 12 -> 63, of which waited for: 10 -> 21; matrix products, arithmetic and copies ran while one was open for 4% -> 8% of each run, Pallas kernels for 0% -> 64%
where the time goes in v1:
time: 1550 us; the launch traced here: 1530 us
  Pallas kernels  1120 us (72%)
  waiting for transfers between devices  130 us (8%)
  starting transfers between devices  100 us (6%)
  local copies, waits for them, and re-layouts  67.3 us (4%)
  matrix products  60.2 us (4%)
  other arithmetic  51.9 us (3%)
    pallas_call x6, Pallas kernels, move_blocks(): pl.pallas_call(kernel, out_shape=out_shapes, in_specs=[pl.BlockSpec(memor...  1120 us
    ppermute x36, waiting for transfers between devices, plane_shift(): return lax.ppermute(value, ('z', 'x', 'core'), pairs)  91.6 us
    ppermute x36, starting transfers between devices, plane_shift(): return lax.ppermute(value, ('z', 'x', 'core'), pairs)  50.9 us
    ppermute x15, waiting for transfers between devices, ring_shift(): return lax.ppermute(value, ('rep', 'y', 'core'), pairs)  38.3 us
  transfers between devices with their start and end apart: 63, of which 21 were waited for; matrix products, arithmetic and copies ran while one was open for 8% of the time, Pallas kernels for 64%

profile of v1, /device:TPU:1, one launch (start us, length us, event | category | flops | bytes accessed | tf_op | source)
XLA Modules:
  0.0 1532.9 jit_solution(14729977117938916740)
XLA Ops:
  20.3 3.4 collective-permute-start.2
  24.4 4.0 collective-permute-done.2
  39.5 17.7 %collective-permute-done.15 = bf16[32,4608]{1,0:T(8,128)(2,1)S(1)} collective-permute-done((bf16[32,4608]{1,0:T(8,128)(2,1)S(1)}, bf16[32,4608]{1,0:T(8,128)(2,1)S(1)}, u32[]{:S(2)}, u32[]{:S(2)}) %collective-permute-start.15) | collective-permute-done | bytes 294944 | tf_op jit(solution)/shard_map/ppermute | solution.py:95
  57.7 3.5 collective-permute-done.5
  61.2 2.7 collective-permute-start.9
  69.3 4.7 collective-permute-done.13
  80.4 264.8 %shard_map.416 = (bf16[16,2,2,16,3072]{4,3,2,1,0:T(8,128)(2,1)}, bf16[16,2,2,16,1024]{4,3,2,1,0:T(8,128)(2,1)}, bf16[16,2,2,16,128]{4,3,2,1,0:T(8,128)(2,1)}) custom-call(s32[34]{0:T(128)} %concatenate.76.index_ref, bf16[4,2,16,4224]{3,2,1,0:T(8,128)(2,1)} %bitcast.201, bf16[4,2,16,4224]{3,2,1,0:T(8,128)(2,1)} %bitcast.208, ...), custom_call_target="tpu_custom_call" | custom-call | bytes 17301504 | tf_op jit(solution)/shard_map/pallas_call | solution.py:141
  346.4 4.6 convolution_bitcast_fusion
  360.3 5.3 collective-permute-done.24
  365.6 5.0 collective-permute-start.11
  372.5 6.2 collective-permute-done.19
  380.2 23.8 %collective-permute-done.20 = bf16[128,4608]{1,0:T(8,128)(2,1)S(1)} collective-permute-done((bf16[128,4608]{1,0:T(8,128)(2,1)}, bf16[128,4608]{1,0:T(8,128)(2,1)S(1)}, u32[]{:S(2)}, u32[]{:S(2)}) %collective-permute-start.20) | collective-permute-done | bytes 1179680 | tf_op jit(solution)/shard_map/ppermute | solution.py:103
  425.6 4.4 collective-permute-start.31
  430.0 287.9 %shard_map.417 = bf16[16,2,32,4608]{3,2,1,0:T(8,128)(2,1)} custom-call(s32[18]{0:T(128)} %concatenate.82.index_ref, bf16[4,32,4608]{2,1,0:T(8,128)(2,1)} %bitcast.198, bf16[4,32,4608]{2,1,0:T(8,128)(2,1)} %bitcast.53.refs_1_, bf16[4,32,4608]{2,1,0:T(8,128)(2,1)} %bitcast.54.refs_2_, bf16[4,32,4608]{2,1,0:T(8,128)(2,1)} %bitcast.55.refs_3_, ...), custom_call_target="tpu_custom_call" | custom-call | bytes 18874368 | tf_op jit(solution)/shard_map/pallas_call | solution.py:141
  718.0 10.1 fusion.12
  729.1 145.0 %shard_map.418 = bf16[16,144,1024]{2,1,0:T(8,128)(2,1)} custom-call(s32[16]{0:T(128)} %stack.246.index_ref, bf16[4,144,1024]{2,1,0:T(8,128)(2,1)} %bitcast.192, bf16[4,144,1024]{2,1,0:T(8,128)(2,1)} %bitcast.202, bf16[4,144,1024]{2,1,0:T(8,128)(2,1)} %bitcast.63.refs_2_, bf16[4,144,1024]{2,1,0:T(8,128)(2,1)} %bitcast.64.refs_3_), custom_call_target="tpu_custom_call" | custom-call | bytes 9437184 | tf_op jit(solution)/shard_map/pallas_call | solution.py:141
  874.2 9.5 multiply_convert_fusion.1
  883.6 8.5 fusion.1
  897.5 8.9 convolution_convert_fusion
  906.4 6.6 dynamic-slice_bitcast_fusion.1
  913.1 2.8 fusion.53
  915.9 2.7 collective-permute-start.44
  918.6 5.4 convolution_convert_fusion.1
  923.9 145.0 %shard_map.421 = (bf16[4,144,1024]{2,1,0:T(8,128)(2,1)}, bf16[4,144,1024]{2,1,0:T(8,128)(2,1)}, bf16[4,144,1024]{2,1,0:T(8,128)(2,1)}, bf16[4,144,1024]{2,1,0:T(8,128)(2,1)}) custom-call(s32[16]{0:T(128)} %stack.263.index_ref, bf16[16,144,1024]{2,1,0:T(8,128)(2,1)} %bitcast.197), custom_call_target="tpu_custom_call" | custom-call | bytes 9437184 | tf_op jit(solution)/shard_map/pallas_call | solution.py:141
  1072.9 2.8 multiply_subtract_fusion.1
  1078.7 3.0 multiply_reduce_fusion.3
  1082.1 3.4 constant_dynamic-slice_fusion.5
  1091.5 2.9 convolution_add_fusion.1
  1094.4 3.8 add_convert_fusion.2
  1100.7 144.9 %shard_map.420 = (bf16[4,32,4608]{2,1,0:T(8,128)(2,1)}, bf16[4,32,4608]{2,1,0:T(8,128)(2,1)}, bf16[4,32,4608]{2,1,0:T(8,128)(2,1)}, bf16[4,32,4608]{2,1,0:T(8,128)(2,1)}) custom-call(s32[16]{0:T(128)} %stack.263.index_ref, bf16[16,32,4608]{2,1,0:T(8,128)(2,1)} %pad_maximum_fusion.1.refs_0_), custom_call_target="tpu_custom_call" | custom-call | bytes 9437184 | tf_op jit(solution)/shard_map/pallas_call | solution.py:141
  1253.2 3.0 add_convert_fusion.3
  1258.4 18.2 %collective-permute-done.47 = bf16[4,32,4608]{2,1,0:T(8,128)(2,1)S(1)} collective-permute-done((bf16[4,32,4608]{2,1,0:T(8,128)(2,1)}, bf16[4,32,4608]{2,1,0:T(8,128)(2,1)S(1)}, u32[]{:S(2)}, u32[]{:S(2)}) %collective-permute-start.47) | collective-permute-done | bytes 1179680 | tf_op jit(solution)/shard_map/ppermute | solution.py:95
  1280.0 5.4 collective-permute-start.49
  1290.8 2.7 collective-permute-done.48
  1293.7 9.7 collective-permute-start.53
  1303.3 3.0 collective-permute-start.52
  1307.9 5.4 collective-permute-done.51
  1313.4 2.7 add_convert_fusion.refs_0_
  1316.1 132.9 %shard_map.419 = (bf16[4,32,4224]{2,1,0:T(8,128)(2,1)}, bf16[4,32,4224]{2,1,0:T(8,128)(2,1)}, bf16[4,32,4224]{2,1,0:T(8,128)(2,1)}, bf16[4,32,4224]{2,1,0:T(8,128)(2,1)}) custom-call(s32[16]{0:T(128)} %stack.263.index_ref, bf16[16,32,4224]{2,1,0:T(8,128)(2,1)} %add_convert_fusion.refs_0_), custom_call_target="tpu_custom_call" | custom-call | bytes 8650752 | tf_op jit(solution)/shard_map/pallas_call | solution.py:141
  1454.8 20.3 %collective-permute-done.36 = bf16[4,32,4224]{2,1,0:T(8,128)(2,1)S(1)} collective-permute-done((bf16[4,32,4224]{2,1,0:T(8,128)(2,1)}, bf16[4,32,4224]{2,1,0:T(8,128)(2,1)S(1)}, u32[]{:S(2)}, u32[]{:S(2)}) %collective-permute-start.36) | collective-permute-done | bytes 1081376 | tf_op jit(solution)/shard_map/ppermute | solution.py:95
  1475.1 3.4 collective-permute-done.34
  1481.6 3.0 collective-permute-start.39
  1488.2 3.0 collective-permute-done.39
  1491.7 3.1 collective-permute-done.37
  1496.7 4.2 collective-permute-start.41
  1503.6 2.8 collective-permute-done.42
  1511.3 2.8 add_add_fusion
  1520.1 3.0 multiply_subtract_fusion.2
  (421 shorter events, 158.2 us)
Async XLA Ops:
  4.8 11.7 collective-permute-start
  13.0 22.0 %collective-permute-start.12 = (bf16[16,4608]{1,0:T(8,128)(2,1)S(1)}, bf16[16,4608]{1,0:T(8,128)(2,1)S(1)}, u32[]{:S(2)}, u32[]{:S(2)}) collective-permute-start(bf16[16,4608]{1,0:T(8,128)(2,1)S(1)} %broadcast_select_fusion.6), channel_id=1, source_target_pairs={{0,1},{1,0},{2,3},{3,2},{4,5},{5,4},{6,7},{7,6},{8,9},{9,8},{10,11... | collective-permute-start | bytes 442376 | tf_op jit(solution)/shard_map/ppermute | solution.py:107
  14.1 24.1 %collective-permute-start.23 = (bf16[72,1024]{1,0:T(8,128)(2,1)S(1)}, bf16[72,1024]{1,0:T(8,128)(2,1)S(1)}, u32[]{:S(2)}, u32[]{:S(2)}) collective-permute-start(bf16[72,1024]{1,0:T(8,128)(2,1)S(1)} %convert_element_type.274), channel_id=1, source_target_pairs={{0,2},{2,0},{1,3},{3,1},{4,6},{6,4},{5,7},{7,5},{8,10},{10,8},{9,1... | collective-permute-start | bytes 442376 | tf_op jit(solution)/shard_map/ppermute | solution.py:111
  30.0 27.2 %collective-permute-start.4 = (bf16[128,4224]{1,0:T(8,128)(2,1)S(1)}, bf16[128,4224]{1,0:T(8,128)(2,1)S(1)}, u32[]{:S(2)}, u32[]{:S(2)}) collective-permute-start(bf16[128,4224]{1,0:T(8,128)(2,1)S(1)} %constant_dynamic-update-slice_fusion), channel_id=1, source_target_pairs={{0,16},{1,5},{4,20},{5,9},{8,24},{9,13},{12,28},{13,1},{16,32},{17... | collective-permute-start | bytes 3244040 | tf_op jit(solution)/shard_map/ppermute | solution.py:95
  31.4 29.8 %collective-permute-start.5 = (bf16[128,4224]{1,0:T(8,128)(2,1)S(1)}, bf16[128,4224]{1,0:T(8,128)(2,1)S(1)}, u32[]{:S(2)}, u32[]{:S(2)}) collective-permute-start(bf16[128,4224]{1,0:T(8,128)(2,1)S(1)} %constant_dynamic-update-slice_fusion), channel_id=1, source_target_pairs={{0,32},{1,9},{4,36},{5,13},{8,40},{9,1},{12,44},{13,5},{16,48},{17... | collective-permute-start | bytes 3244040 | tf_op jit(solution)/shard_map/ppermute | solution.py:95
  33.7 30.5 %collective-permute-start.6 = (bf16[128,4224]{1,0:T(8,128)(2,1)S(1)}, bf16[128,4224]{1,0:T(8,128)(2,1)S(1)}, u32[]{:S(2)}, u32[]{:S(2)}) collective-permute-start(bf16[128,4224]{1,0:T(8,128)(2,1)S(1)} %constant_dynamic-update-slice_fusion), channel_id=1, source_target_pairs={{0,48},{1,13},{4,52},{5,1},{8,56},{9,5},{12,60},{13,9},{16,0},{17,... | collective-permute-start | bytes 3244040 | tf_op jit(solution)/shard_map/ppermute | solution.py:95
  35.1 22.1 %collective-permute-start.15 = (bf16[32,4608]{1,0:T(8,128)(2,1)S(1)}, bf16[32,4608]{1,0:T(8,128)(2,1)S(1)}, u32[]{:S(2)}, u32[]{:S(2)}) collective-permute-start(bf16[32,4608]{1,0:T(8,128)(2,1)S(1)} %pad_maximum_fusion.18), channel_id=1, source_target_pairs={{0,12},{1,49},{4,0},{5,53},{8,4},{9,57},{12,8},{13,61},{16,28},{17... | collective-permute-start | bytes 884744 | tf_op jit(solution)/shard_map/ppermute | solution.py:95
  38.2 28.5 %collective-permute-start.14 = (bf16[32,4608]{1,0:T(8,128)(2,1)S(1)}, bf16[32,4608]{1,0:T(8,128)(2,1)S(1)}, u32[]{:S(2)}, u32[]{:S(2)}) collective-permute-start(bf16[32,4608]{1,0:T(8,128)(2,1)S(1)} %pad_maximum_fusion.18), channel_id=1, source_target_pairs={{0,8},{1,33},{4,12},{5,37},{8,0},{9,41},{12,4},{13,45},{16,24},{17... | collective-permute-start | bytes 884744 | tf_op jit(solution)/shard_map/ppermute | solution.py:95
  57.2 18.4 %collective-permute-start.7 = (bf16[128,4224]{1,0:T(8,128)(2,1)S(1)}, bf16[128,4224]{1,0:T(8,128)(2,1)S(1)}, u32[]{:S(2)}, u32[]{:S(2)}) collective-permute-start(bf16[128,4224]{1,0:T(8,128)(2,1)S(1)} %constant_dynamic-update-slice_fusion), channel_id=1, source_target_pairs={{0,1},{1,0},{2,3},{3,2},{4,5},{5,4},{6,7},{7,6},{8,9},{9,8},{10,11... | collective-permute-start | bytes 3244040 | tf_op jit(solution)/shard_map/ppermute | solution.py:107
  57.2 19.3 %collective-permute-start.8 = (bf16[128,4224]{1,0:T(8,128)(2,1)S(1)}, bf16[128,4224]{1,0:T(8,128)(2,1)S(1)}, u32[]{:S(2)}, u32[]{:S(2)}) collective-permute-start(bf16[128,4224]{1,0:T(8,128)(2,1)S(1)} %collective-permute-done.4), channel_id=1, source_target_pairs={{0,1},{1,0},{2,3},{3,2},{4,5},{5,4},{6,7},{7,6},{8,9},{9,8},{10,11... | collective-permute-start | bytes 3244040 | tf_op jit(solution)/shard_map/ppermute | solution.py:107
  61.2 16.5 %collective-permute-start.9 = (bf16[128,4224]{1,0:T(8,128)(2,1)S(1)}, bf16[128,4224]{1,0:T(8,128)(2,1)S(1)}, u32[]{:S(2)}, u32[]{:S(2)}) collective-permute-start(bf16[128,4224]{1,0:T(8,128)(2,1)S(1)} %collective-permute-done.5), channel_id=1, source_target_pairs={{0,1},{1,0},{2,3},{3,2},{4,5},{5,4},{6,7},{7,6},{8,9},{9,8},{10,11... | collective-permute-start | bytes 3244040 | tf_op jit(solution)/shard_map/ppermute | solution.py:107
  64.1 14.7 collective-permute-start.10
  74.0 279.1 %collective-permute-start.26 = (bf16[144,1024]{1,0:T(8,128)(2,1)}, bf16[144,1024]{1,0:T(8,128)(2,1)S(1)}, u32[]{:S(2)}, u32[]{:S(2)}) collective-permute-start(bf16[144,1024]{1,0:T(8,128)(2,1)} %pad_maximum_fusion.19), channel_id=1, source_target_pairs={{0,12},{1,49},{4,0},{5,53},{8,4},{9,57},{12,8},{13,61},{16,28},{17... | collective-permute-start | bytes 884744 | tf_op jit(solution)/shard_map/ppermute | solution.py:95
  75.6 282.7 %collective-permute-start.25 = (bf16[144,1024]{1,0:T(8,128)(2,1)}, bf16[144,1024]{1,0:T(8,128)(2,1)S(1)}, u32[]{:S(2)}, u32[]{:S(2)}) collective-permute-start(bf16[144,1024]{1,0:T(8,128)(2,1)} %pad_maximum_fusion.19), channel_id=1, source_target_pairs={{0,8},{1,33},{4,12},{5,37},{8,0},{9,41},{12,4},{13,45},{16,24},{17... | collective-permute-start | bytes 884744 | tf_op jit(solution)/shard_map/ppermute | solution.py:95
  76.5 277.9 %collective-permute-start.16 = (bf16[128,4608]{1,0:T(8,128)(2,1)S(1)}, bf16[128,4608]{1,0:T(8,128)(2,1)}, u32[]{:S(2)}, u32[]{:S(2)}) collective-permute-start(bf16[128,4608]{1,0:T(8,128)(2,1)S(1)} %pad_maximum_fusion.6), channel_id=1, source_target_pairs={{0,16},{1,5},{4,20},{5,9},{8,24},{9,13},{12,28},{13,1},{16,32},{17... | collective-permute-start | bytes 3538952 | tf_op jit(solution)/shard_map/ppermute | solution.py:95
  77.7 278.0 %collective-permute-start.17 = (bf16[128,4608]{1,0:T(8,128)(2,1)S(1)}, bf16[128,4608]{1,0:T(8,128)(2,1)}, u32[]{:S(2)}, u32[]{:S(2)}) collective-permute-start(bf16[128,4608]{1,0:T(8,128)(2,1)S(1)} %pad_maximum_fusion.6), channel_id=1, source_target_pairs={{0,32},{1,9},{4,36},{5,13},{8,40},{9,1},{12,44},{13,5},{16,48},{17... | collective-permute-start | bytes 3538952 | tf_op jit(solution)/shard_map/ppermute | solution.py:95
  78.8 278.3 %collective-permute-start.18 = (bf16[128,4608]{1,0:T(8,128)(2,1)S(1)}, bf16[128,4608]{1,0:T(8,128)(2,1)}, u32[]{:S(2)}, u32[]{:S(2)}) collective-permute-start(bf16[128,4608]{1,0:T(8,128)(2,1)S(1)} %pad_maximum_fusion.6), channel_id=1, source_target_pairs={{0,48},{1,13},{4,52},{5,1},{8,56},{9,5},{12,60},{13,9},{16,0},{17,... | collective-permute-start | bytes 3538952 | tf_op jit(solution)/shard_map/ppermute | solution.py:95
  353.0 25.7 %collective-permute-start.19 = (bf16[128,4608]{1,0:T(8,128)(2,1)S(1)}, bf16[128,4608]{1,0:T(8,128)(2,1)S(1)}, u32[]{:S(2)}, u32[]{:S(2)}) collective-permute-start(bf16[128,4608]{1,0:T(8,128)(2,1)S(1)} %pad_maximum_fusion.6), channel_id=1, source_target_pairs={{0,2},{1,3},{2,64},{3,65},{64,66},{65,67},{66,0},{67,1},{4,6},{5,7... | collective-permute-start | bytes 3538952 | tf_op jit(solution)/shard_map/ppermute | solution.py:103
  354.4 49.6 %collective-permute-start.20 = (bf16[128,4608]{1,0:T(8,128)(2,1)}, bf16[128,4608]{1,0:T(8,128)(2,1)S(1)}, u32[]{:S(2)}, u32[]{:S(2)}) collective-permute-start(bf16[128,4608]{1,0:T(8,128)(2,1)} %collective-permute-done.16), channel_id=1, source_target_pairs={{0,2},{1,3},{2,64},{3,65},{64,66},{65,67},{66,0},{67,1},{4,6},{5,7... | collective-permute-start | bytes 3538952 | tf_op jit(solution)/shard_map/ppermute | solution.py:103
  355.7 49.9 %collective-permute-start.21 = (bf16[128,4608]{1,0:T(8,128)(2,1)}, bf16[128,4608]{1,0:T(8,128)(2,1)S(1)}, u32[]{:S(2)}, u32[]{:S(2)}) collective-permute-start(bf16[128,4608]{1,0:T(8,128)(2,1)} %collective-permute-done.17), channel_id=1, source_target_pairs={{0,66},{1,67},{2,0},{3,1},{64,2},{65,3},{66,64},{67,65},{4,70},{5,... | collective-permute-start | bytes 3538952 | tf_op jit(solution)/shard_map/ppermute | solution.py:103
  357.1 68.5 %collective-permute-start.22 = (bf16[128,4608]{1,0:T(8,128)(2,1)}, bf16[128,4608]{1,0:T(8,128)(2,1)}, u32[]{:S(2)}, u32[]{:S(2)}) collective-permute-start(bf16[128,4608]{1,0:T(8,128)(2,1)} %collective-permute-done.18), channel_id=1, source_target_pairs={{0,66},{1,67},{2,0},{3,1},{64,2},{65,3},{66,64},{67,65},{4,70},{5,... | collective-permute-start | bytes 3538952 | tf_op jit(solution)/shard_map/ppermute | solution.py:103
  365.6 352.3 %collective-permute-start.11 = (bf16[256,1024]{1,0:T(8,128)(2,1)}, bf16[256,1024]{1,0:T(8,128)(2,1)}, u32[]{:S(2)}, u32[]{:S(2)}) collective-permute-start(bf16[256,1024]{1,0:T(8,128)(2,1)} %multiply_convert_fusion.6), channel_id=1, source_target_pairs={{0,1},{1,0},{2,3},{3,2},{4,5},{5,4},{6,7},{7,6},{8,9},{9,8},{10,11... | collective-permute-start | bytes 1572872 | tf_op jit(solution)/shard_map/ppermute | solution.py:107
  378.7 349.4 %collective-permute-start.27 = (bf16[576,1024]{1,0:T(8,128)(2,1)S(1)}, bf16[576,1024]{1,0:T(8,128)(2,1)S(1)}, u32[]{:S(2)}, u32[]{:S(2)}) collective-permute-start(bf16[576,1024]{1,0:T(8,128)(2,1)S(1)} %pad_maximum_fusion.7), channel_id=1, source_target_pairs={{0,16},{1,5},{4,20},{5,9},{8,24},{9,13},{12,28},{13,1},{16,32},{17... | collective-permute-start | bytes 3538952 | tf_op jit(solution)/shard_map/ppermute | solution.py:95
  404.0 324.1 %collective-permute-start.28 = (bf16[576,1024]{1,0:T(8,128)(2,1)S(1)}, bf16[576,1024]{1,0:T(8,128)(2,1)}, u32[]{:S(2)}, u32[]{:S(2)}) collective-permute-start(bf16[576,1024]{1,0:T(8,128)(2,1)S(1)} %pad_maximum_fusion.7), channel_id=1, source_target_pairs={{0,32},{1,9},{4,36},{5,13},{8,40},{9,1},{12,44},{13,5},{16,48},{17... | collective-permute-start | bytes 3538952 | tf_op jit(solution)/shard_map/ppermute | solution.py:95
  405.7 322.5 %collective-permute-start.29 = (bf16[576,1024]{1,0:T(8,128)(2,1)S(1)}, bf16[576,1024]{1,0:T(8,128)(2,1)}, u32[]{:S(2)}, u32[]{:S(2)}) collective-permute-start(bf16[576,1024]{1,0:T(8,128)(2,1)S(1)} %pad_maximum_fusion.7), channel_id=1, source_target_pairs={{0,48},{1,13},{4,52},{5,1},{8,56},{9,5},{12,60},{13,9},{16,0},{17,... | collective-permute-start | bytes 3538952 | tf_op jit(solution)/shard_map/ppermute | solution.py:95
  425.6 448.5 %collective-permute-start.31 = (bf16[256,1024]{1,0:T(8,128)(2,1)}, bf16[256,1024]{1,0:T(8,128)(2,1)}, u32[]{:S(2)}, u32[]{:S(2)}) collective-permute-start(bf16[256,1024]{1,0:T(8,128)(2,1)} %fusion.10), channel_id=1, source_target_pairs={{0,1},{1,0},{2,3},{3,2},{4,5},{5,4},{6,7},{7,6},{8,9},{9,8},{10,11... | collective-permute-start | bytes 1572872 | tf_op jit(solution)/shard_map/ppermute | solution.py:107
  893.0 176.9 %collective-permute-start.32 = (bf16[256,1024]{1,0:T(8,128)(2,1)}, bf16[256,1024]{1,0:T(8,128)(2,1)}, u32[]{:S(2)}, u32[]{:S(2)}) collective-permute-start(bf16[256,1024]{1,0:T(8,128)(2,1)} %slice.271), channel_id=1, source_target_pairs={{0,1},{1,0},{2,3},{3,2},{4,5},{5,4},{6,7},{7,6},{8,9},{9,8},{10,11... | collective-permute-start | bytes 1572872 | tf_op jit(solution)/shard_map/ppermute | solution.py:107
  896.6 175.6 %collective-permute-start.30 = (bf16[256,1024]{1,0:T(8,128)(2,1)}, bf16[256,1024]{1,0:T(8,128)(2,1)}, u32[]{:S(2)}, u32[]{:S(2)}) collective-permute-start(bf16[256,1024]{1,0:T(8,128)(2,1)} %slice.272), channel_id=1, source_target_pairs={{0,1},{1,0},{2,3},{3,2},{4,5},{5,4},{6,7},{7,6},{8,9},{9,8},{10,11... | collective-permute-start | bytes 1572872 | tf_op jit(solution)/shard_map/ppermute | solution.py:107
  915.9 178.5 %collective-permute-start.43 = (bf16[16,32,2304]{2,1,0:T(8,128)(2,1)}, bf16[16,32,2304]{2,1,0:T(8,128)(2,1)}, u32[]{:S(2)}, u32[]{:S(2)}) collective-permute-start(bf16[16,32,2304]{2,1,0:T(8,128)(2,1)} %get-tuple-element.226), channel_id=1, source_target_pairs={{0,2},{1,3},{2,64},{3,65},{64,66},{65,67},{66,0},{67,1},{4,6},{5,7... | collective-permute-start | bytes 7077896 | tf_op jit(solution)/shard_map/ppermute | solution.py:103
  915.9 178.5 %collective-permute-start.44 = (bf16[16,32,2304]{2,1,0:T(8,128)(2,1)}, bf16[16,32,2304]{2,1,0:T(8,128)(2,1)}, u32[]{:S(2)}, u32[]{:S(2)}) collective-permute-start(bf16[16,32,2304]{2,1,0:T(8,128)(2,1)} %get-tuple-element.227), channel_id=1, source_target_pairs={{0,66},{1,67},{2,0},{3,1},{64,2},{65,3},{66,64},{67,65},{4,70},{5,... | collective-permute-start | bytes 7077896 | tf_op jit(solution)/shard_map/ppermute | solution.py:103
  1068.9 179.8 %collective-permute-start.56 = (bf16[4,144,1024]{2,1,0:T(8,128)(2,1)}, bf16[4,144,1024]{2,1,0:T(8,128)(2,1)}, u32[]{:S(2)}, u32[]{:S(2)}) collective-permute-start(bf16[4,144,1024]{2,1,0:T(8,128)(2,1)} %get-tuple-element.60), channel_id=1, source_target_pairs={{0,48},{1,13},{4,52},{5,1},{8,56},{9,5},{12,60},{13,9},{16,0},{17,... | collective-permute-start | bytes 3538952 | tf_op jit(solution)/shard_map/ppermute | solution.py:95
  1069.9 180.9 %collective-permute-start.55 = (bf16[4,144,1024]{2,1,0:T(8,128)(2,1)}, bf16[4,144,1024]{2,1,0:T(8,128)(2,1)}, u32[]{:S(2)}, u32[]{:S(2)}) collective-permute-start(bf16[4,144,1024]{2,1,0:T(8,128)(2,1)} %get-tuple-element.59), channel_id=1, source_target_pairs={{0,32},{1,9},{4,36},{5,13},{8,40},{9,1},{12,44},{13,5},{16,48},{17... | collective-permute-start | bytes 3538952 | tf_op jit(solution)/shard_map/ppermute | solution.py:95
  1072.2 181.0 %collective-permute-start.54 = (bf16[4,144,1024]{2,1,0:T(8,128)(2,1)}, bf16[4,144,1024]{2,1,0:T(8,128)(2,1)}, u32[]{:S(2)}, u32[]{:S(2)}) collective-permute-start(bf16[4,144,1024]{2,1,0:T(8,128)(2,1)} %get-tuple-element.58), channel_id=1, source_target_pairs={{0,16},{1,5},{4,20},{5,9},{8,24},{9,13},{12,28},{13,1},{16,32},{17... | collective-permute-start | bytes 3538952 | tf_op jit(solution)/shard_map/ppermute | solution.py:95
  1245.5 31.0 %collective-permute-start.47 = (bf16[4,32,4608]{2,1,0:T(8,128)(2,1)}, bf16[4,32,4608]{2,1,0:T(8,128)(2,1)S(1)}, u32[]{:S(2)}, u32[]{:S(2)}) collective-permute-start(bf16[4,32,4608]{2,1,0:T(8,128)(2,1)} %get-tuple-element.56), channel_id=1, source_target_pairs={{0,48},{1,13},{4,52},{5,1},{8,56},{9,5},{12,60},{13,9},{16,0},{17,... | collective-permute-start | bytes 3538952 | tf_op jit(solution)/shard_map/ppermute | solution.py:95
  1247.9 28.7 %collective-permute-start.46 = (bf16[4,32,4608]{2,1,0:T(8,128)(2,1)}, bf16[4,32,4608]{2,1,0:T(8,128)(2,1)S(1)}, u32[]{:S(2)}, u32[]{:S(2)}) collective-permute-start(bf16[4,32,4608]{2,1,0:T(8,128)(2,1)} %get-tuple-element.55), channel_id=1, source_target_pairs={{0,32},{1,9},{4,36},{5,13},{8,40},{9,1},{12,44},{13,5},{16,48},{17... | collective-permute-start | bytes 3538952 | tf_op jit(solution)/shard_map/ppermute | solution.py:95
  1248.7 28.9 %collective-permute-start.45 = (bf16[4,32,4608]{2,1,0:T(8,128)(2,1)}, bf16[4,32,4608]{2,1,0:T(8,128)(2,1)S(1)}, u32[]{:S(2)}, u32[]{:S(2)}) collective-permute-start(bf16[4,32,4608]{2,1,0:T(8,128)(2,1)} %get-tuple-element.54), channel_id=1, source_target_pairs={{0,16},{1,5},{4,20},{5,9},{8,24},{9,13},{12,28},{13,1},{16,32},{17... | collective-permute-start | bytes 3538952 | tf_op jit(solution)/shard_map/ppermute | solution.py:95
  1250.8 62.6 %collective-permute-start.33 = (bf16[16,32,4224]{2,1,0:T(8,128)(2,1)S(1)}, bf16[16,32,4224]{2,1,0:T(8,128)(2,1)S(1)}, u32[]{:S(2)}, u32[]{:S(2)}) collective-permute-start(bf16[16,32,4224]{2,1,0:T(8,128)(2,1)S(1)} %pad_maximum_fusion.2), channel_id=1, source_target_pairs={{0,1},{1,0},{2,3},{3,2},{4,5},{5,4},{6,7},{7,6},{8,9},{9,8},{10,11... | collective-permute-start | bytes 12976136 | tf_op jit(solution)/shard_map/ppermute | solution.py:107
  1256.3 23.7 %collective-permute-start.59 = (bf16[144,1024]{1,0:T(8,128)(2,1)S(1)}, bf16[144,1024]{1,0:T(8,128)(2,1)S(1)}, u32[]{:S(2)}, u32[]{:S(2)}) collective-permute-start(bf16[144,1024]{1,0:T(8,128)(2,1)S(1)} %get-tuple-element.231), channel_id=1, source_target_pairs={{0,12},{1,49},{4,0},{5,53},{8,4},{9,57},{12,8},{13,61},{16,28},{17... | collective-permute-start | bytes 884744 | tf_op jit(solution)/shard_map/ppermute | solution.py:95
  1280.0 10.3 collective-permute-start.49
  1286.8 19.6 %collective-permute-start.61 = (bf16[72,1024]{1,0:T(8,128)(2,1)S(1)}, bf16[72,1024]{1,0:T(8,128)(2,1)S(1)}, u32[]{:S(2)}, u32[]{:S(2)}) collective-permute-start(bf16[72,1024]{1,0:T(8,128)(2,1)S(1)} %get-tuple-element.246), channel_id=1, source_target_pairs={{0,66},{1,67},{2,0},{3,1},{64,2},{65,3},{66,64},{67,65},{4,70},{5,... | collective-permute-start | bytes 442376 | tf_op jit(solution)/shard_map/ppermute | solution.py:103
  1287.1 19.6 %collective-permute-start.60 = (bf16[72,1024]{1,0:T(8,128)(2,1)S(1)}, bf16[72,1024]{1,0:T(8,128)(2,1)S(1)}, u32[]{:S(2)}, u32[]{:S(2)}) collective-permute-start(bf16[72,1024]{1,0:T(8,128)(2,1)S(1)} %get-tuple-element.246), channel_id=1, source_target_pairs={{0,2},{1,3},{2,64},{3,65},{64,66},{65,67},{66,0},{67,1},{4,6},{5,7... | collective-permute-start | bytes 442376 | tf_op jit(solution)/shard_map/ppermute | solution.py:103
  1290.3 13.0 collective-permute-start.62
  1293.7 19.7 %collective-permute-start.53 = (bf16[16,4608]{1,0:T(8,128)(2,1)S(1)}, bf16[16,4608]{1,0:T(8,128)(2,1)S(1)}, u32[]{:S(2)}, u32[]{:S(2)}) collective-permute-start(bf16[16,4608]{1,0:T(8,128)(2,1)S(1)} %get-tuple-element.252), channel_id=1, source_target_pairs={{0,65},{1,64},{2,67},{3,66},{64,1},{65,0},{66,3},{67,2},{4,69},{5,... | collective-permute-start | bytes 442376 | tf_op jit(solution)/shard_map/ppermute | solution.py:103
  1449.1 26.0 %collective-permute-start.36 = (bf16[4,32,4224]{2,1,0:T(8,128)(2,1)}, bf16[4,32,4224]{2,1,0:T(8,128)(2,1)S(1)}, u32[]{:S(2)}, u32[]{:S(2)}) collective-permute-start(bf16[4,32,4224]{2,1,0:T(8,128)(2,1)} %get-tuple-element.52), channel_id=1, source_target_pairs={{0,48},{1,13},{4,52},{5,1},{8,56},{9,5},{12,60},{13,9},{16,0},{17,... | collective-permute-start | bytes 3244040 | tf_op jit(solution)/shard_map/ppermute | solution.py:95
  1451.1 24.0 %collective-permute-start.35 = (bf16[4,32,4224]{2,1,0:T(8,128)(2,1)}, bf16[4,32,4224]{2,1,0:T(8,128)(2,1)}, u32[]{:S(2)}, u32[]{:S(2)}) collective-permute-start(bf16[4,32,4224]{2,1,0:T(8,128)(2,1)} %get-tuple-element.51), channel_id=1, source_target_pairs={{0,32},{1,9},{4,36},{5,13},{8,40},{9,1},{12,44},{13,5},{16,48},{17... | collective-permute-start | bytes 3244040 | tf_op jit(solution)/shard_map/ppermute | solution.py:95
  1451.1 27.4 %collective-permute-start.34 = (bf16[4,32,4224]{2,1,0:T(8,128)(2,1)}, bf16[4,32,4224]{2,1,0:T(8,128)(2,1)}, u32[]{:S(2)}, u32[]{:S(2)}) collective-permute-start(bf16[4,32,4224]{2,1,0:T(8,128)(2,1)} %get-tuple-element.50), channel_id=1, source_target_pairs={{0,16},{1,5},{4,20},{5,9},{8,24},{9,13},{12,28},{13,1},{16,32},{17... | collective-permute-start | bytes 3244040 | tf_op jit(solution)/shard_map/ppermute | solution.py:95
  1484.6 10.3 collective-permute-start.37
  1496.7 11.1 collective-permute-start.41
  (109 other events, 2441.8 us)
